TPU v7x, 128 devices: a whole 4x4x4 slice. The times are simulated.
128 devices in a mesh: gz: 4 (over z), xy: 32 (over x, y, core).
Axes of the slice: x: 4, y: 4, z: 4, core: 2. Of those that a mesh axis runs over, the one named last changes fastest.
Arguments:
- areas: bfloat16 [262144, 512], P(('gz', 'xy')), may hold values from 0 to 1
- angles: float32 [2, 262144], P(None, ('gz', 'xy')), may hold values from -3.140625 to 3.140625
- transm: float32 [262144], P(('gz', 'xy')), may hold values from 0.1 to 1
- owner: int32 [262144, 1], P(('gz', 'xy')), may hold values from 0 to 127; in each aligned block of 2048 rows (0 to 2047, 2048 to 4095, ...) at most 24 rows name the same one
- tile: int32 [262144], P(('gz', 'xy')), may hold values from 0 to 511
- live_count: int32 [128], P(('gz', 'xy')), may hold values from 1024 to 2048, as said below
- rock: float32 [32, 512, 2048], P('gz', 'xy'), may hold values from 0.5 to 2
- source: float32 [32, 512, 2048], P('gz', 'xy'), may hold values from -6 to 6
- start: float32 [32, 512, 2048], P('gz', 'xy'), may hold values from -6 to 6
Outputs:
- perm: float32 [6, 32, 512, 2048], P(None, 'gz', 'xy')
- pressure: float32 [32, 512, 2048], P('gz', 'xy')
Inputs may be any that keep to these rules, and one draw needn't show every extreme that they name: Within the rows of one device no owner is named more than 24 times, a bound that some block reaches. `live_count`: some device has exactly 2048 live rows.
All inputs are finite; a program needn't handle non-finite values.
Results may differ from a plain program's by a relative error of at most 0.0015.
Values may be sent and summed in bfloat16 or wider, within the bound.
A program may use at most 192 MiB of HBM per device.

v0:
```python
import functools
import math

import jax
import jax.numpy as jnp
import numpy as np
from jax import lax
from jax.experimental import pallas as pl
from jax.experimental.pallas import tpu as pltpu
from jax.sharding import PartitionSpec as P

TILE = 8
SWEEPS = 2
CAP = 24
CELLS = TILE * TILE * TILE
LANES = 128
STEP_WEIGHTS = (
    1.0 / (1.0 - 0.7 * math.cos(math.pi / 4)),
    1.0 / (1.0 + 0.7 * math.cos(math.pi / 4)),
)
MESH = pl.DeviceIdType.MESH
F32 = jnp.float32
BF16 = jnp.bfloat16


SIZES = (4, 4, 4, 2)
TOTAL = 128
GROUPS = 8
OTHERS = 16
SEND_STEPS = 16
RECV_STEPS = (32, 32, 32, 16, 16)
DEPTH = max(RECV_STEPS) * CAP
CUTS = CELLS // LANES
HALVES = 2
BANDS = 2
SOME = 4
STEPS = len(STEP_WEIGHTS) * SWEEPS


def rem(value, by):
    return lax.rem(value, jnp.int32(by))


def div(value, by):
    return lax.div(value, jnp.int32(by))


def place():
    gz, xy = lax.axis_index("gz"), lax.axis_index("xy")
    return gz, div(xy, 8), rem(div(xy, 2), 4), rem(xy, 2)


def offset_of(step):
    core, rest = step % 2, step // 2
    a, b, c = rest % 4, (rest // 4) % 4, rest // 16
    return a, (3 * a + b) % 4, (a + 2 * b + c) % 4, core


def partner(me, step):
    core, rest = rem(step, 2), div(step, 2)
    a, b, c = rem(rest, 4), rem(div(rest, 4), 4), div(rest, 16)
    x, y = rem(me[1] + 3 * a + b, 4), rem(me[2] + a + 2 * b + c, 4)
    return rem(me[0] + a, 4), x * 8 + y * 2 + rem(me[3] + core, 2)


def near_partner(me, u):
    return rem(me[0] + div(u, 2), 4), me[1] * 8 + me[2] * 2 + rem(me[3] + rem(u, 2), 2)


def far_partner(me, w):
    return me[0], rem(me[1] + div(w, 4), 4) * 8 + rem(me[2] + rem(w, 4), 4) * 2 + me[3]


def permutations():
    first, second, third = [np.zeros((TOTAL, TOTAL), np.float32) for _ in range(3)]
    for step in range(TOTAL):
        dz, dx, dy, dc = offset_of(step)
        u, w = dz * 2 + dc, dx * 4 + dy
        first[u * OTHERS + w, step] = 1
        second[w * GROUPS + u, u * OTHERS + w] = 1
        third[w * GROUPS + u, step] = 1
    return [jnp.asarray(m, BF16) for m in (first, second, third)]


def dot(a, b):
    return jnp.dot(a, b, preferred_element_type=F32)


def iota(shape, dim):
    return lax.broadcasted_iota(jnp.int32, shape, dim)


def loop(first, last, body, unroll=1):
    def step(n, carry):
        body(n)
        return carry

    lax.fori_loop(first, last, step, 0, unroll=unroll)


def row_facts(me, angles, transm, owner, tile, live):
    rows = owner.shape[1]
    dz = ((owner >> 5) - me[0]) & 3
    dx = ((owner >> 3) - me[1]) & 3
    dy = ((owner >> 1) - me[2]) & 3
    dc = (owner - me[3]) & 1
    b = (dx - 3 * dz) & 3
    c = (dy - dz - 2 * b) & 3
    step = ((c * 4 + b) * 4 + dz) * 2 + dc
    step = jnp.where(iota((1, rows), 1) < live, step, -1)
    sines, cosines = jnp.sin(angles), jnp.cos(angles)
    polar_sin = sines[0:1]
    normal_x = polar_sin * cosines[1:2]
    normal_y = polar_sin * sines[1:2]
    normal_z = cosines[0:1]
    facts = [
        transm * (1.0 - normal_x * normal_x),
        transm * (1.0 - normal_y * normal_y),
        transm * (1.0 - normal_z * normal_z),
        -transm * normal_x * normal_y,
        -transm * normal_x * normal_z,
        -transm * normal_y * normal_z,
        (tile >> 8).astype(F32),
        (tile & 255).astype(F32),
    ]
    marks = (step == iota((TOTAL, rows), 0)).astype(F32)
    width = 256
    upper = (iota((width, width), 0) <= iota((width, width), 1)).astype(BF16)
    carry = jnp.zeros((TOTAL, 1), F32)
    ranks = []
    for block in range(rows // width):
        part = marks[:, block * width : (block + 1) * width]
        running = dot(part.astype(BF16), upper) + carry
        carry = running[:, width - 1 : width]
        ranks.append(jnp.sum(running * part, axis=0, keepdims=True) - 1.0)
    rank = jnp.concatenate(ranks, axis=1)
    slot = jnp.where(step >= 0, step.astype(F32) * CAP + rank, -1.0)
    chosen = (rank == iota((32, rows), 0).astype(F32)).astype(F32)
    spread = jnp.concatenate([chosen * fact for fact in facts], axis=0).astype(BF16)
    sheet = lax.dot_general(
        marks.astype(BF16), spread, (((1,), (1,)), ((), ())), preferred_element_type=F32
    )
    return slot, sheet


def swap_groups(values):
    lane = iota(values[0].shape, 1)
    for size in (4, 2, 1):
        high = (lane // (16 * size)) % 2 == 1
        other = jnp.where(high, lane - 16 * size, lane + 16 * size)
        result = list(values)
        for i in range(8):
            if i & size == 0:
                low, up = values[i], values[i + size]
                crossed = jnp.take_along_axis(jnp.where(high, low, up), other, axis=1)
                result[i] = jnp.where(high, crossed, low)
                result[i + size] = jnp.where(high, up, crossed)
        values = result
    return values


def split_lanes(values):
    lane = iota(values[0].shape, 1)
    index = (lane % 16) * 8 + lane // 16
    return swap_groups([jnp.take_along_axis(value, index, axis=1) for value in values])


def join_lanes(values):
    lane = iota(values[0].shape, 1)
    index = (lane % 8) * 16 + lane // 8
    return [jnp.take_along_axis(value, index, axis=1) for value in swap_groups(values)]


def lanes_of(half, m):
    return slice((half * 8 + m) * LANES, (half * 8 + m + 1) * LANES)


def along_x(rows, first, last):
    shape = rows.shape
    rows = rows.reshape(shape[0], 8, 8, LANES)
    lane, l = iota(first.shape, 2), iota(rows.shape, 2)
    edge = jnp.zeros((1,) + first.shape[1:], F32)
    over = pltpu.roll(first, LANES - 1, 2)
    over = jnp.where(lane == LANES - 1, jnp.concatenate([over[1:], edge], axis=0), over)
    under = pltpu.roll(last, 1, 2)
    under = jnp.where(lane == 0, jnp.concatenate([edge, under[:-1]], axis=0), under)
    over = jnp.stack([pltpu.roll(over, 7 - k, 1) if k < 7 else over for k in range(8)], axis=1)
    under = jnp.stack([pltpu.roll(under, 8 - k, 1) if k else under for k in range(8)], axis=1)
    more = jnp.where(l == 7, over, pltpu.roll(rows, 7, 2))
    less = jnp.where(l == 0, under, pltpu.roll(rows, 1, 2))
    return more.reshape(shape), less.reshape(shape)


def along_x_faces(rows):
    lane, l = iota(rows.shape, 3), iota(rows.shape, 2)
    edge = jnp.zeros((rows.shape[0], 1) + rows.shape[2:], F32)
    up, down = pltpu.roll(rows, 7, 2), pltpu.roll(rows, 1, 2)
    over = pltpu.roll(up, LANES - 1, 3)
    over = jnp.where(lane == LANES - 1, jnp.concatenate([over[:, 1:], edge], axis=1), over)
    under = pltpu.roll(down, 1, 3)
    under = jnp.where(lane == 0, jnp.concatenate([edge, under[:, :-1]], axis=1), under)
    return jnp.where(l == 7, over, up), jnp.where(l == 0, under, down)


def at8(start, size):
    return pl.ds(start if isinstance(start, int) else pl.multiple_of(start, 8), size)


def kernel(
    angles_ref,
    transm_ref,
    owner_ref,
    tile_ref,
    live_ref,
    first_ref,
    second_ref,
    third_ref,
    areas_hbm,
    rock_hbm,
    source_hbm,
    start_hbm,
    perm_ref,
    pressure_ref,
    areas_ref,
    plain_ref,
    slot_ref,
    picked_ref,
    send_ref,
    recv_ref,
    near_out,
    near_in,
    far_out,
    far_in,
    turned_ref,
    column_ref,
    cell_ref,
    flip_ref,
    acc_ref,
    rock_ref,
    source_ref,
    p_ref,
    d_ref,
    g_ref,
    coef_ref,
    yy_ref,
    zz_ref,
    field_ref,
    load_sem,
    send_sem,
    recv_sem,
    near_send,
    near_recv,
    far_send,
    far_recv,
    halo_send,
    halo_recv,
    coef_send,
    coef_recv,
):
    me = place()
    z, h = lax.axis_index("gz"), lax.axis_index("xy")
    gz_count, xy_count = 4, 32
    nz, ny = plain_ref.shape[1], plain_ref.shape[2]

    loads = [
        pltpu.make_async_copy(source, target, load_sem.at[n])
        for n, (source, target) in enumerate((
            (areas_hbm, areas_ref),
            (rock_hbm, plain_ref.at[0]),
            (source_hbm, plain_ref.at[1]),
            (start_hbm, plain_ref.at[2]),
        ))
    ]
    for load in loads:
        load.start()

    barrier = pltpu.get_barrier_semaphore()
    loop(
        1,
        TOTAL,
        lambda step: pl.semaphore_signal(
            barrier, inc=1, device_id=partner(me, step), device_id_type=MESH
        ),
    )

    slot, sheet = row_facts(
        me, angles_ref[...], transm_ref[...], owner_ref[...], tile_ref[...], live_ref[...]
    )
    slot_ref[...] = slot
    near_out[...] = dot(first_ref[...], sheet.astype(BF16)).reshape(near_out.shape)
    rows = areas_ref.shape[0]

    def pick(chunk):
        base = chunk * SEND_STEPS
        wanted = (iota((SEND_STEPS * CAP, rows), 0) + base * CAP).astype(F32)
        chosen = (slot_ref[...] == wanted).astype(F32).astype(BF16)
        picked_ref[...] = dot(chosen, areas_ref[...])

        def pack(index):
            block = picked_ref[at8(index * CAP, CAP), :]
            parts = [block[:, c * LANES : (c + 1) * LANES] for c in range(CUTS)]
            send_ref[base + index] = jnp.concatenate(parts, axis=0).astype(BF16)

        loop(0, SEND_STEPS, pack, unroll=4)

    def send(step, part):
        pltpu.make_async_remote_copy(
            send_ref.at[step],
            recv_ref.at[step],
            send_sem,
            recv_sem.at[part],
            device_id=partner(me, step),
            device_id_type=MESH,
        ).start()

    def near_copy(u):
        pltpu.make_async_remote_copy(
            near_out.at[u],
            near_in.at[u],
            near_send,
            near_recv,
            device_id=near_partner(me, u),
            device_id_type=MESH,
        ).start()

    def far_copy(w):
        pltpu.make_async_remote_copy(
            far_out.at[w],
            far_in.at[w],
            far_send,
            far_recv,
            device_id=far_partner(me, w),
            device_id_type=MESH,
        ).start()

    def drain(ref, first, count, sem):
        part = ref.at[pl.ds(first, count)]
        pltpu.make_async_copy(part, part, sem).wait()

    loads[0].wait()
    pick(0)
    pl.semaphore_wait(barrier, TOTAL - 1)
    loop(1, SEND_STEPS, lambda step: send(step, 0))
    recv_ref[0] = send_ref[0]
    loop(1, GROUPS, near_copy)
    near_in[0] = near_out[0]

    def pick_and_send(chunk, part):
        pick(chunk)
        loop(0, SEND_STEPS, lambda index: send(chunk * SEND_STEPS + index, part))

    pick_and_send(1, 0)
    loop(2, 4, lambda chunk: pick_and_send(chunk, div(chunk, 2)))
    drain(near_in, 1, GROUPS - 1, near_recv)
    swapped = dot(second_ref[...], near_in[...].reshape(TOTAL, 256).astype(BF16))
    far_out[...] = swapped.reshape(far_out.shape)
    loop(1, OTHERS, far_copy)
    far_in[0] = far_out[0]
    loop(4, 6, lambda chunk: pick_and_send(chunk, div(chunk, 2)))
    loop(6, 8, lambda chunk: pick_and_send(chunk, chunk - 3))

    for load in loads[1:]:
        load.wait()

    def split(i):
        for n in range(3):
            spots = [(b, half) for b in range(BANDS) for half in range(HALVES)]
            pieces = []
            for m in range(8):
                parts = [plain_ref[n, i, b * 8 : (b + 1) * 8, lanes_of(half, m)] for b, half in spots]
                pieces.append(jnp.concatenate(parts, axis=0))
            for l, value in enumerate(split_lanes(pieces)):
                for k, (b, half) in enumerate(spots):
                    here = value[k * 8 : (k + 1) * 8]
                    if n == 2:
                        p_ref[0, 1 + i, half, pl.ds(8 + b * 64 + l, 8, stride=8), :] = here
                    else:
                        target = (rock_ref, source_ref)[n]
                        target[i, half, pl.ds(b * 64 + l, 8, stride=8), :] = here

    loop(0, nz, split)

    def beside(dz, dh):
        return (z + dz + gz_count) % gz_count, (h + dh + xy_count) % xy_count

    sides = [(dz, dh) for dz in (-1, 0, 1) for dh in (-1, 0, 1) if dz or dh]

    def planes(d, halo):
        if d == 0:
            return pl.ds(1, nz)
        if halo:
            return pl.ds(0, 1) if d > 0 else pl.ds(nz + 1, 1)
        return pl.ds(nz, 1) if d > 0 else pl.ds(1, 1)

    def lines(d, halo):
        if d == 0:
            return pl.ds(8, ny * 8)
        if halo:
            return pl.ds(0, 8) if d > 0 else pl.ds(ny * 8 + 8, 8)
        return pl.ds(ny * 8, 8) if d > 0 else pl.ds(8, 8)

    def halo_copy(t, n):
        dz, dh = sides[n]
        return pltpu.make_async_remote_copy(
            p_ref.at[t, planes(dz, False), :, lines(dh, False)],
            p_ref.at[t, planes(dz, True), :, lines(dh, True)],
            halo_send.at[t, n],
            halo_recv.at[t, n],
            device_id=beside(dz, dh),
            device_id_type=MESH,
        )

    for n in range(len(sides)):
        halo_copy(0, n).start()

    drain(far_in, 1, OTHERS - 1, far_recv)
    turned_ref[...] = dot(
        jnp.transpose(far_in[...].reshape(TOTAL, 256)).astype(BF16), third_ref[...]
    )
    acc_ref[...] = jnp.zeros_like(acc_ref)
    pieces = acc_ref.shape[0] // 6

    def add_rows(base, count):
        depth = count * CAP
        lined = pltpu.roll(turned_ref[...], (TOTAL - base) % TOTAL, 1)
        for index in range(count):
            part = lined[:, index : index + 1]
            where = slice(index * CAP, (index + 1) * CAP)
            for v in range(6):
                column_ref[v, where, :] = jnp.broadcast_to(part[32 * v : 32 * v + CAP], (CAP, LANES))
            number = part[192 : 192 + CAP] * 256.0 + part[224 : 224 + CAP]
            column_ref[6, where, :] = jnp.broadcast_to(number, (CAP, LANES))

        def unpack(index):
            block = recv_ref[base + index].astype(F32)
            for c in range(CUTS):
                cell_ref[c, at8(index * CAP, CAP), :] = block[c * CAP : (c + 1) * CAP]

        loop(0, count, unpack, unroll=4)
        for c in range(CUTS):
            flip_ref[c * LANES : (c + 1) * LANES, :depth] = jnp.transpose(cell_ref[c, :depth]).astype(BF16)

        def component(q):
            lane = iota((depth, LANES), 1).astype(F32)
            number = column_ref[6, :depth]
            value = column_ref[q, :depth]
            parts = [
                jnp.where(number == lane + part * LANES, value, 0.0).astype(BF16)
                for part in range(pieces)
            ]
            product = dot(flip_ref[:, :depth], jnp.concatenate(parts, axis=1))
            for part in range(pieces):
                acc_ref[q * pieces + part] += product[:, part * LANES : (part + 1) * LANES]

        loop(0, 6, component)

    base = 0
    for part, count in enumerate(RECV_STEPS):
        first = 1 if part == 0 else 0
        drain(recv_ref, base + first, count - first, recv_sem.at[part])
        add_rows(base, count)
        base += count

    def fill(n):
        i, b = div(n, BANDS), rem(n, BANDS)
        rock = rock_ref[i, :, at8(b * 64, 64), :]
        for q in range(3):
            where = pl.ds((q * BANDS + b) * HALVES, HALVES)
            value = acc_ref[where, at8(i * 64, 64), :] + rock
            acc_ref[where, at8(i * 64, 64), :] = value
            if q == 1:
                yy_ref[i, :, at8(8 + b * 64, 64), :] = value
            if q == 2:
                zz_ref[1 + i, :, at8(b * 64, 64), :] = value

    loop(0, nz * BANDS, fill)
    coef_copies = []
    for d in (1, -1):
        ends = [
            (yy_ref.at[:, :, lines(d, False)], yy_ref.at[:, :, lines(d, True)], (0, d)),
            (zz_ref.at[planes(d, False)], zz_ref.at[planes(d, True)], (d, 0)),
        ]
        for source, target, side in ends:
            n = len(coef_copies)
            coef_copies.append(
                pltpu.make_async_remote_copy(
                    source,
                    target,
                    coef_send.at[n],
                    coef_recv.at[n],
                    device_id=beside(*side),
                    device_id_type=MESH,
                )
            )
    for copy in coef_copies:
        copy.start()

    def join(i):
        per = BANDS * HALVES
        for q in range(0, 6, 2):
            values = join_lanes([
                acc_ref[q * per : (q + 2) * per, pl.ds(i * 64 + l, 8, stride=8), :].reshape(16 * per, LANES)
                for l in range(8)
            ])
            for k in range(2 * per):
                b, half = (k % per) // HALVES, k % HALVES
                for m, value in enumerate(values):
                    perm_ref[q + k // per, i, b * 8 : (b + 1) * 8, lanes_of(half, m)] = value[k * 8 : (k + 1) * 8]

    loop(0, nz, join)
    for copy in coef_copies:
        copy.wait()

    def clear(ref, index):
        ref[index] = jnp.zeros_like(ref[index])

    every = slice(None)
    low, high = slice(0, 8), slice(ny * 8 + 8, ny * 8 + 16)
    inside = slice(1, nz + 1)

    @pl.when(z == 0)
    def _():
        clear(zz_ref, 0)

    @pl.when(z == gz_count - 1)
    def _():
        clear(zz_ref, nz + 1)

    @pl.when(h == 0)
    def _():
        clear(yy_ref, (every, every, low))

    @pl.when(h == xy_count - 1)
    def _():
        clear(yy_ref, (every, every, high))

    def prepare(n):
        i, b = div(n, BANDS), rem(n, BANDS)
        here = at8(b * 64, 64)
        where = pl.ds(b * HALVES, HALVES)
        k = acc_ref[where, at8(i * 64, 64), :]
        first = acc_ref[where, pl.ds(i * 64, 8, stride=8), :]
        last = acc_ref[where, pl.ds(i * 64 + 7, 8, stride=8), :]
        more, less = along_x(k, first, last)
        faces = [0.5 * (k + more), 0.5 * (k + less)]
        k = yy_ref[i, :, at8(b * 64 + 8, 64), :]
        faces += [0.5 * (k + yy_ref[i, :, at8(b * 64 + 16, 64), :]), 0.5 * (k + yy_ref[i, :, here, :])]
        k = zz_ref[1 + i, :, here, :]
        faces += [0.5 * (k + zz_ref[2 + i, :, here, :]), 0.5 * (k + zz_ref[i, :, here, :])]
        inverse = 1.0 / functools.reduce(lambda left, right: left + right, faces)
        for m, face in enumerate(faces):
            coef_ref[m, i, :, here, :] = face * inverse
        for m in range(3):
            cross = acc_ref[pl.ds(((3 + m) * BANDS + b) * HALVES, HALVES), at8(i * 64, 64), :]
            coef_ref[6 + m, i, :, here, :] = cross * (0.25 * inverse)
        coef_ref[9, i, :, here, :] = source_ref[i, :, here, :] * inverse

    loop(0, nz * BANDS, prepare)

    for t, weight in enumerate(STEP_WEIGHTS * SWEEPS):

        def rows_along_x(i, b, t=t):
            start = 8 + b * 64
            rows = p_ref[t, i, :, at8(start, 64), :]
            first = p_ref[t, i, :, pl.ds(start, 8, stride=8), :]
            last = p_ref[t, i, :, pl.ds(start + 7, 8, stride=8), :]
            return along_x(rows, first, last)

        def inner(i):
            for b in range(BANDS):
                here = slice(b * 64, b * 64 + 64)
                more, less = rows_along_x(1 + i, b)
                d_ref[1 + i, :, 8 + b * 64 : 72 + b * 64, :] = more - less
                g_ref[i, :, here, :] = (
                    coef_ref[9, i, :, here, :]
                    + coef_ref[0, i, :, here, :] * more
                    + coef_ref[1, i, :, here, :] * less
                )

        def advance(n, t=t, weight=weight):
            i, y = div(n, ny // SOME), rem(n, ny // SOME) * SOME
            here = at8(y * 8, SOME * 8)
            p = lambda dz, dy: p_ref[t, i + 1 + dz, :, at8((y + 1 + dy) * 8, SOME * 8), :]
            d = lambda dz, dy: d_ref[i + 1 + dz, :, at8((y + 1 + dy) * 8, SOME * 8), :]
            coef = lambda m: coef_ref[m, i, :, here, :]
            total = g_ref[i, :, here, :]
            total = total + coef(2) * p(0, 1) + coef(3) * p(0, -1)
            total = total + coef(4) * p(1, 0) + coef(5) * p(-1, 0)
            total = total + coef(6) * (d(0, 1) - d(0, -1)) + coef(7) * (d(1, 0) - d(-1, 0))
            total = total + coef(8) * ((p(1, 1) - p(-1, 1)) - (p(1, -1) - p(-1, -1)))
            value = (1.0 - weight) * p(0, 0) + weight * total
            if t + 1 < STEPS:
                p_ref[t + 1, i + 1, :, at8(y * 8 + 8, SOME * 8), :] = value
            else:
                field_ref[i, :, here, :] = value

        per = ny // SOME
        loop(0, nz, inner)
        for n, side in enumerate(sides):
            if side[0] == 0:
                halo_copy(t, n).wait()

        @pl.when(h == 0)
        def _():
            clear(p_ref, (t, inside, every, low))

        @pl.when(h == xy_count - 1)
        def _():
            clear(p_ref, (t, inside, every, high))

        for line in (low, high):
            more, less = along_x_faces(p_ref[t, inside, :, line, :])
            d_ref[inside, :, line, :] = more - less
        loop(per, (nz - 1) * per, advance)
        for n, side in enumerate(sides):
            if side[0] != 0:
                halo_copy(t, n).wait()

        @pl.when(h == 0)
        def _():
            clear(p_ref, (t, 0, every, low))
            clear(p_ref, (t, nz + 1, every, low))

        @pl.when(h == xy_count - 1)
        def _():
            clear(p_ref, (t, 0, every, high))
            clear(p_ref, (t, nz + 1, every, high))

        @pl.when(z == 0)
        def _():
            clear(p_ref, (t, 0))

        @pl.when(z == gz_count - 1)
        def _():
            clear(p_ref, (t, nz + 1))

        for i in (0, nz + 1):
            for b in range(BANDS):
                more, less = rows_along_x(i, b)
                d_ref[i, :, 8 + b * 64 : 72 + b * 64, :] = more - less
        loop(0, per, advance)
        loop((nz - 1) * per, nz * per, advance)
        if t + 1 < STEPS:
            for n in range(len(sides)):
                halo_copy(t + 1, n).start()

    def finish(i):
        spots = [(b, half) for b in range(BANDS) for half in range(HALVES)]
        values = join_lanes([
            jnp.concatenate([field_ref[i, half, pl.ds(b * 64 + l, 8, stride=8), :] for b, half in spots], axis=0)
            for l in range(8)
        ])
        for k, (b, half) in enumerate(spots):
            for m, value in enumerate(values):
                pressure_ref[i, b * 8 : (b + 1) * 8, lanes_of(half, m)] = value[k * 8 : (k + 1) * 8]

    loop(0, nz, finish)
    drain(send_ref, 1, TOTAL - 1, send_sem)
    drain(near_out, 1, GROUPS - 1, near_send)
    drain(far_out, 1, OTHERS - 1, far_send)


def body(areas, angles, transm, owner, tile, live_count, rock, source, start):
    rows = areas.shape[0]
    nz, ny, nx = rock.shape
    lines = ny * 8
    vmem = pl.BlockSpec(memory_space=pltpu.VMEM)
    anywhere = pl.BlockSpec(memory_space=pl.ANY)
    block = (TOTAL, CAP * CUTS, LANES)
    brick = (nz, HALVES, lines, LANES)
    dma = pltpu.SemaphoreType.DMA
    perm, pressure = pl.pallas_call(
        kernel,
        out_shape=[
            jax.ShapeDtypeStruct((6, nz, ny, nx), F32),
            jax.ShapeDtypeStruct((nz, ny, nx), F32),
        ],
        in_specs=[vmem] * 8 + [anywhere] * 4,
        out_specs=[vmem, vmem],
        scratch_shapes=[
            pltpu.VMEM((rows, CELLS), BF16),
            pltpu.VMEM((3, nz, ny, nx), F32),
            pltpu.VMEM((1, rows), F32),
            pltpu.VMEM((SEND_STEPS * CAP, CELLS), F32),
            pltpu.VMEM(block, BF16),
            pltpu.VMEM(block, BF16),
            pltpu.VMEM((GROUPS, OTHERS, 256), F32),
            pltpu.VMEM((GROUPS, OTHERS, 256), F32),
            pltpu.VMEM((OTHERS, GROUPS, 256), F32),
            pltpu.VMEM((OTHERS, GROUPS, 256), F32),
            pltpu.VMEM((256, TOTAL), F32),
            pltpu.VMEM((7, DEPTH, LANES), F32),
            pltpu.VMEM((CUTS, DEPTH, LANES), F32),
            pltpu.VMEM((CELLS, DEPTH), BF16),
            pltpu.VMEM((6 * BANDS * HALVES, CELLS, LANES), F32),
            pltpu.VMEM(brick, F32),
            pltpu.VMEM(brick, F32),
            pltpu.VMEM((STEPS, nz + 2, HALVES, lines + 16, LANES), F32),
            pltpu.VMEM((nz + 2, HALVES, lines + 16, LANES), F32),
            pltpu.VMEM(brick, F32),
            pltpu.VMEM((10,) + brick, F32),
            pltpu.VMEM((nz, HALVES, lines + 16, LANES), F32),
            pltpu.VMEM((nz + 2, HALVES, lines, LANES), F32),
            pltpu.VMEM(brick, F32),
            dma((4,)),
            dma,
            dma((len(RECV_STEPS),)),
            dma,
            dma,
            dma,
            dma,
            dma((STEPS, 8)),
            dma((STEPS, 8)),
            dma((4,)),
            dma((4,)),
        ],
        compiler_params=pltpu.CompilerParams(
            collective_id=0, has_side_effects=True, vmem_limit_bytes=62 << 20
        ),
    )(
        angles,
        transm.reshape(1, rows),
        owner.reshape(1, rows),
        tile.reshape(1, rows),
        live_count.reshape(1, 1),
        *permutations(),
        areas,
        rock,
        source,
        start,
    )
    return perm, pressure


def solution(mesh):
    return jax.shard_map(
        body,
        mesh=mesh,
        in_specs=(
            P(("gz", "xy"), None),
            P(None, ("gz", "xy")),
            P(("gz", "xy")),
            P(("gz", "xy"), None),
            P(("gz", "xy")),
            P(("gz", "xy")),
            P("gz", "xy", None),
            P("gz", "xy", None),
            P("gz", "xy", None),
        ),
        out_specs=(P(None, "gz", "xy", None), P("gz", "xy", None)),
        check_vma=False,
    )
```

profile of v0, /device:TPU:1, one launch (start us, length us, event | category | flops | bytes accessed | tf_op | source)
XLA Modules:
  0.0 114.2 jit_solution(5507411246972186797)
XLA Ops:
  1.3 105.5 %shard_map.131 = (f32[6,8,16,2048]{3,2,1,0:T(8,128)}, f32[8,16,2048]{2,1,0:T(8,128)}) custom-call(f32[2,2048]{1,0:T(2,128)} %angles_ref.1, f32[1,2048]{1,0:T(1,128)} %bitcast.5, s32[1,2048]{1,0:T(1,128)} %bitcast.6, s32[1,2048]{1,0:T(1,128)} %bitcast.7, s32[1,1]{1,0:T(1,128)} %bitcast.4.live_ref, bf16[128,128]{1,0:T(8,128)(2,1)} %constant.6.clone.first_ref, ...), custom_call_target="tpu_custom_call" | custom-call | tf_op jit(solution)/shard_map/pallas_call | solution.py:672
  106.8 0.0 copy-start
  106.8 6.4 %copy.17 = f32[6,8,16,2048]{3,2,1,0:T(8,128)} copy(f32[6,8,16,2048]{3,2,1,0:T(8,128)} %get-tuple-element.4) | data formatting | bytes 12582912
  113.2 0.0 copy-done
  113.2 1.0 copy.18
Async XLA Ops:
  106.8 6.4 %copy-start = (f32[8,16,2048]{2,1,0:T(8,128)S(1)}, f32[8,16,2048]{2,1,0:T(8,128)}, u32[]{:S(2)}) copy-start(f32[8,16,2048]{2,1,0:T(8,128)} %get-tuple-element.5) | copy-start | bytes 3145732
where the time goes:
time: 114 us
  Pallas kernels  106 us (93%)
  local copies, waits for them, and re-layouts  7.35 us (6%)
  between operations  1.3 us (1%)
    pallas_call x1, Pallas kernels, body(): pl.pallas_call(kernel, out_shape=[jax.ShapeDtypeStruct((6, nz, ny, nx), F...  106 us
    unnamed x4, local copies, waits for them, and re-layouts  7.35 us

commit v1 on v0

--- a/solution.py
+++ b/solution.py
@@ -98,7 +98,7 @@
     lax.fori_loop(first, last, step, 0, unroll=unroll)
 
 
-def row_facts(me, angles, transm, owner, tile, live):
+def row_slots(me, owner, live):
     rows = owner.shape[1]
     dz = ((owner >> 5) - me[0]) & 3
     dx = ((owner >> 3) - me[1]) & 3
@@ -108,6 +108,21 @@
     c = (dy - dz - 2 * b) & 3
     step = ((c * 4 + b) * 4 + dz) * 2 + dc
     step = jnp.where(iota((1, rows), 1) < live, step, -1)
+    marks = (step == iota((TOTAL, rows), 0)).astype(F32)
+    width = 256
+    upper = (iota((width, width), 0) <= iota((width, width), 1)).astype(BF16)
+    carry = jnp.zeros((TOTAL, 1), F32)
+    ranks = []
+    for block in range(rows // width):
+        part = marks[:, block * width : (block + 1) * width]
+        running = dot(part.astype(BF16), upper) + carry
+        carry = running[:, width - 1 : width]
+        ranks.append(jnp.sum(running * part, axis=0, keepdims=True) - 1.0)
+    return step.astype(F32), jnp.concatenate(ranks, axis=1)
+
+
+def fact_sheet(step, rank, angles, transm, tile):
+    rows = step.shape[1]
     sines, cosines = jnp.sin(angles), jnp.cos(angles)
     polar_sin = sines[0:1]
     normal_x = polar_sin * cosines[1:2]
@@ -123,24 +138,10 @@
         (tile >> 8).astype(F32),
         (tile & 255).astype(F32),
     ]
-    marks = (step == iota((TOTAL, rows), 0)).astype(F32)
-    width = 256
-    upper = (iota((width, width), 0) <= iota((width, width), 1)).astype(BF16)
-    carry = jnp.zeros((TOTAL, 1), F32)
-    ranks = []
-    for block in range(rows // width):
-        part = marks[:, block * width : (block + 1) * width]
-        running = dot(part.astype(BF16), upper) + carry
-        carry = running[:, width - 1 : width]
-        ranks.append(jnp.sum(running * part, axis=0, keepdims=True) - 1.0)
-    rank = jnp.concatenate(ranks, axis=1)
-    slot = jnp.where(step >= 0, step.astype(F32) * CAP + rank, -1.0)
+    marks = (step == iota((TOTAL, rows), 0).astype(F32)).astype(F32).astype(BF16)
     chosen = (rank == iota((32, rows), 0).astype(F32)).astype(F32)
     spread = jnp.concatenate([chosen * fact for fact in facts], axis=0).astype(BF16)
-    sheet = lax.dot_general(
-        marks.astype(BF16), spread, (((1,), (1,)), ((), ())), preferred_element_type=F32
-    )
-    return slot, sheet
+    return lax.dot_general(marks, spread, (((1,), (1,)), ((), ())), preferred_element_type=F32)
 
 
 def swap_groups(values):
@@ -219,6 +220,8 @@
     rock_hbm,
     source_hbm,
     start_hbm,
+    perm_out,
+    pressure_out,
     perm_ref,
     pressure_ref,
     areas_ref,
@@ -256,6 +259,8 @@
     halo_recv,
     coef_send,
     coef_recv,
+    ready_sem,
+    out_sem,
 ):
     me = place()
     z, h = lax.axis_index("gz"), lax.axis_index("xy")
@@ -275,25 +280,22 @@
         load.start()
 
     barrier = pltpu.get_barrier_semaphore()
-    loop(
-        1,
-        TOTAL,
-        lambda step: pl.semaphore_signal(
-            barrier, inc=1, device_id=partner(me, step), device_id_type=MESH
-        ),
-    )
-
-    slot, sheet = row_facts(
-        me, angles_ref[...], transm_ref[...], owner_ref[...], tile_ref[...], live_ref[...]
-    )
-    slot_ref[...] = slot
-    near_out[...] = dot(first_ref[...], sheet.astype(BF16)).reshape(near_out.shape)
+
+    def greet(sem, to):
+        pl.semaphore_signal(sem, inc=1, device_id=to, device_id_type=MESH)
+
+    loop(1, GROUPS, lambda u: greet(barrier, near_partner(me, u)))
+    loop(1, OTHERS, lambda w: greet(barrier, far_partner(me, w)))
+    step, rank = row_slots(me, owner_ref[...], live_ref[...])
+    slot_ref[0:1] = jnp.where(step >= 0, step * CAP + rank, -1.0)
+    slot_ref[1:2] = step
+    slot_ref[2:3] = rank
     rows = areas_ref.shape[0]
 
     def pick(chunk):
         base = chunk * SEND_STEPS
         wanted = (iota((SEND_STEPS * CAP, rows), 0) + base * CAP).astype(F32)
-        chosen = (slot_ref[...] == wanted).astype(F32).astype(BF16)
+        chosen = (slot_ref[0:1] == wanted).astype(F32).astype(BF16)
         picked_ref[...] = dot(chosen, areas_ref[...])
 
         def pack(index):
@@ -337,26 +339,30 @@
         part = ref.at[pl.ds(first, count)]
         pltpu.make_async_copy(part, part, sem).wait()
 
+    pl.semaphore_wait(barrier, GROUPS + OTHERS - 2)
+    loop(1, OTHERS, lambda w: greet(ready_sem, far_partner(me, w)))
     loads[0].wait()
     pick(0)
-    pl.semaphore_wait(barrier, TOTAL - 1)
+    sheet = fact_sheet(
+        slot_ref[1:2], slot_ref[2:3], angles_ref[...], transm_ref[...], tile_ref[...]
+    )
+    near_out[...] = dot(first_ref[...], sheet.astype(BF16)).reshape(near_out.shape)
+    pl.semaphore_wait(ready_sem, OTHERS - 1)
+    loop(1, GROUPS, near_copy)
+    near_in[0] = near_out[0]
     loop(1, SEND_STEPS, lambda step: send(step, 0))
     recv_ref[0] = send_ref[0]
-    loop(1, GROUPS, near_copy)
-    near_in[0] = near_out[0]
-
     def pick_and_send(chunk, part):
         pick(chunk)
         loop(0, SEND_STEPS, lambda index: send(chunk * SEND_STEPS + index, part))
 
     pick_and_send(1, 0)
-    loop(2, 4, lambda chunk: pick_and_send(chunk, div(chunk, 2)))
     drain(near_in, 1, GROUPS - 1, near_recv)
     swapped = dot(second_ref[...], near_in[...].reshape(TOTAL, 256).astype(BF16))
     far_out[...] = swapped.reshape(far_out.shape)
     loop(1, OTHERS, far_copy)
     far_in[0] = far_out[0]
-    loop(4, 6, lambda chunk: pick_and_send(chunk, div(chunk, 2)))
+    loop(2, 6, lambda chunk: pick_and_send(chunk, div(chunk, 2)))
     loop(6, 8, lambda chunk: pick_and_send(chunk, chunk - 3))
 
     for load in loads[1:]:
@@ -420,8 +426,7 @@
     acc_ref[...] = jnp.zeros_like(acc_ref)
     pieces = acc_ref.shape[0] // 6
 
-    def add_rows(base, count):
-        depth = count * CAP
+    def list_columns(base, count):
         lined = pltpu.roll(turned_ref[...], (TOTAL - base) % TOTAL, 1)
         for index in range(count):
             part = lined[:, index : index + 1]
@@ -430,6 +435,9 @@
                 column_ref[v, where, :] = jnp.broadcast_to(part[32 * v : 32 * v + CAP], (CAP, LANES))
             number = part[192 : 192 + CAP] * 256.0 + part[224 : 224 + CAP]
             column_ref[6, where, :] = jnp.broadcast_to(number, (CAP, LANES))
+
+    def add_rows(base, count):
+        depth = count * CAP
 
         def unpack(index):
             block = recv_ref[base + index].astype(F32)
@@ -452,11 +460,12 @@
             for part in range(pieces):
                 acc_ref[q * pieces + part] += product[:, part * LANES : (part + 1) * LANES]
 
-        loop(0, 6, component)
+        loop(0, 6, component, unroll=2)
 
     base = 0
     for part, count in enumerate(RECV_STEPS):
         first = 1 if part == 0 else 0
+        list_columns(base, count)
         drain(recv_ref, base + first, count - first, recv_sem.at[part])
         add_rows(base, count)
         base += count
@@ -495,19 +504,24 @@
     for copy in coef_copies:
         copy.start()
 
-    def join(i):
+    def join(i, q):
         per = BANDS * HALVES
-        for q in range(0, 6, 2):
-            values = join_lanes([
-                acc_ref[q * per : (q + 2) * per, pl.ds(i * 64 + l, 8, stride=8), :].reshape(16 * per, LANES)
-                for l in range(8)
-            ])
-            for k in range(2 * per):
-                b, half = (k % per) // HALVES, k % HALVES
-                for m, value in enumerate(values):
-                    perm_ref[q + k // per, i, b * 8 : (b + 1) * 8, lanes_of(half, m)] = value[k * 8 : (k + 1) * 8]
-
-    loop(0, nz, join)
+        values = join_lanes([
+            acc_ref[q * per : (q + 2) * per, pl.ds(i * 64 + l, 8, stride=8), :].reshape(16 * per, LANES)
+            for l in range(8)
+        ])
+        for k in range(2 * per):
+            b, half = (k % per) // HALVES, k % HALVES
+            for m, value in enumerate(values):
+                perm_ref[q + k // per, i, b * 8 : (b + 1) * 8, lanes_of(half, m)] = value[k * 8 : (k + 1) * 8]
+
+    out_copies = [
+        pltpu.make_async_copy(perm_ref.at[q : q + 2], perm_out.at[q : q + 2], out_sem.at[q // 2])
+        for q in (0, 2, 4)
+    ] + [pltpu.make_async_copy(pressure_ref, pressure_out, out_sem.at[3])]
+    loop(0, nz, lambda i: join(i, 0))
+    out_copies[0].start()
+    loop(0, nz // 2, lambda i: join(i, 2))
     for copy in coef_copies:
         copy.wait()
 
@@ -596,6 +610,8 @@
 
         per = ny // SOME
         loop(0, nz, inner)
+        if t:
+            loop(t * 2 - 2, t * 2, lambda i: join(i, 4))
         for n, side in enumerate(sides):
             if side[0] == 0:
                 halo_copy(t, n).wait()
@@ -612,6 +628,13 @@
             more, less = along_x_faces(p_ref[t, inside, :, line, :])
             d_ref[inside, :, line, :] = more - less
         loop(per, (nz - 1) * per, advance)
+        if t == 1:
+            loop(nz // 2, nz, lambda i: join(i, 2))
+            out_copies[1].start()
+        if t == 2:
+            loop(nz - 2, nz, lambda i: join(i, 4))
+        if t == 3:
+            out_copies[2].start()
         for n, side in enumerate(sides):
             if side[0] != 0:
                 halo_copy(t, n).wait()
@@ -655,9 +678,22 @@
                 pressure_ref[i, b * 8 : (b + 1) * 8, lanes_of(half, m)] = value[k * 8 : (k + 1) * 8]
 
     loop(0, nz, finish)
+    out_copies[3].start()
+    for copy in out_copies:
+        copy.wait()
     drain(send_ref, 1, TOTAL - 1, send_sem)
     drain(near_out, 1, GROUPS - 1, near_send)
     drain(far_out, 1, OTHERS - 1, far_send)
+
+
+def export_kernel(perm_ref, pressure_ref, perm_out, pressure_out, sems):
+    copies = [
+        pltpu.make_async_copy(perm_ref.at[q], perm_out.at[q], sems.at[q]) for q in range(6)
+    ] + [pltpu.make_async_copy(pressure_ref, pressure_out, sems.at[6])]
+    for copy in copies:
+        copy.start()
+    for copy in copies:
+        copy.wait()
 
 
 def body(areas, angles, transm, owner, tile, live_count, rock, source, start):
@@ -676,11 +712,13 @@
             jax.ShapeDtypeStruct((nz, ny, nx), F32),
         ],
         in_specs=[vmem] * 8 + [anywhere] * 4,
-        out_specs=[vmem, vmem],
+        out_specs=[anywhere, anywhere],
         scratch_shapes=[
+            pltpu.VMEM((6, nz, ny, nx), F32),
+            pltpu.VMEM((nz, ny, nx), F32),
             pltpu.VMEM((rows, CELLS), BF16),
             pltpu.VMEM((3, nz, ny, nx), F32),
-            pltpu.VMEM((1, rows), F32),
+            pltpu.VMEM((8, rows), F32),
             pltpu.VMEM((SEND_STEPS * CAP, CELLS), F32),
             pltpu.VMEM(block, BF16),
             pltpu.VMEM(block, BF16),
@@ -713,6 +751,8 @@
             dma((STEPS, 8)),
             dma((4,)),
             dma((4,)),
+            pltpu.SemaphoreType.REGULAR,
+            dma((4,)),
         ],
         compiler_params=pltpu.CompilerParams(
             collective_id=0, has_side_effects=True, vmem_limit_bytes=62 << 20
@@ -729,7 +769,16 @@
         source,
         start,
     )
-    return perm, pressure
+    return tuple(
+        pl.pallas_call(
+            export_kernel,
+            out_shape=[jax.ShapeDtypeStruct(value.shape, F32) for value in (perm, pressure)],
+            in_specs=[anywhere, anywhere],
+            out_specs=[anywhere, anywhere],
+            scratch_shapes=[dma((7,))],
+            compiler_params=pltpu.CompilerParams(vmem_limit_bytes=62 << 20),
+        )(perm, pressure)
+    )
 
 
 def solution(mesh):

time: 114 us -> 322 us (2.82)
  Pallas kernels: 106 us -> 320 us
  local copies, waits for them, and re-layouts: 7.35 us -> 0 us
    pallas_call x0 -> x1, Pallas kernels: none -> 224 us  [body(): pl.pallas_call(export_kernel, out_shape=[jax.ShapeDtypeStruct(value.shape...]
    pallas_call x1, Pallas kernels: 106 us -> 96.7 us  [body(): pl.pallas_call(kernel, out_shape=[jax.ShapeDtypeStruct((6, nz, ny, nx), F...]
    unnamed x4 -> x0, local copies, waits for them, and re-layouts: 7.35 us -> none
where the time goes in v1:
time: 322 us
  Pallas kernels  320 us (99%)
    pallas_call x1, Pallas kernels, body(): pl.pallas_call(export_kernel, out_shape=[jax.ShapeDtypeStruct(value.shape...  224 us
    pallas_call x1, Pallas kernels, body(): pl.pallas_call(kernel, out_shape=[jax.ShapeDtypeStruct((6, nz, ny, nx), F...  96.7 us

profile of v1, /device:TPU:1, one launch (start us, length us, event | category | flops | bytes accessed | tf_op | source)
XLA Modules:
  0.0 321.6 jit_solution(13037791442891796972)
XLA Ops:
  1.3 96.7 %shard_map.131 = (f32[6,8,16,2048]{3,2,1,0:T(8,128)}, f32[8,16,2048]{2,1,0:T(8,128)}) custom-call(f32[2,2048]{1,0:T(2,128)} %angles_ref.1, f32[1,2048]{1,0:T(1,128)} %bitcast.5, s32[1,2048]{1,0:T(1,128)} %bitcast.6, s32[1,2048]{1,0:T(1,128)} %bitcast.7, s32[1,1]{1,0:T(1,128)} %bitcast.4.live_ref, bf16[128,128]{1,0:T(8,128)(2,1)} %constant.6.clone.first_ref, ...), custom_call_target="tpu_custom_call" | custom-call | tf_op jit(solution)/shard_map/pallas_call | solution.py:708
  97.9 223.5 %shard_map.132 = (f32[6,8,16,2048]{3,2,1,0:T(8,128)}, f32[8,16,2048]{2,1,0:T(8,128)}) custom-call(f32[6,8,16,2048]{3,2,1,0:T(8,128)} %get-tuple-element.4.perm_ref, f32[8,16,2048]{2,1,0:T(8,128)} %get-tuple-element.5.pressure_ref), custom_call_target="tpu_custom_call" | custom-call | tf_op jit(solution)/shard_map/pallas_call | solution.py:773

commit v2 on v1

v2 whole, which is shorter than its diff:
```python
import functools
import math

import jax
import jax.numpy as jnp
import numpy as np
from jax import lax
from jax.experimental import pallas as pl
from jax.experimental.pallas import tpu as pltpu
from jax.sharding import PartitionSpec as P

TILE = 8
SWEEPS = 2
CAP = 24
CELLS = TILE * TILE * TILE
LANES = 128
STEP_WEIGHTS = (
    1.0 / (1.0 - 0.7 * math.cos(math.pi / 4)),
    1.0 / (1.0 + 0.7 * math.cos(math.pi / 4)),
)
MESH = pl.DeviceIdType.MESH
F32 = jnp.float32
BF16 = jnp.bfloat16


SIZES = (4, 4, 4, 2)
TOTAL = 128
GROUPS = 8
OTHERS = 16
SEND_STEPS = 16
RECV_STEPS = (32, 32, 32, 16, 16)
DEPTH = max(RECV_STEPS) * CAP
CUTS = CELLS // LANES
HALVES = 2
BANDS = 2
SOME = 4
LIMIT = 56
STEPS = len(STEP_WEIGHTS) * SWEEPS


def rem(value, by):
    return lax.rem(value, jnp.int32(by))


def div(value, by):
    return lax.div(value, jnp.int32(by))


def place():
    gz, xy = lax.axis_index("gz"), lax.axis_index("xy")
    return gz, div(xy, 8), rem(div(xy, 2), 4), rem(xy, 2)


def offset_of(step):
    core, rest = step % 2, step // 2
    a, b, c = rest % 4, (rest // 4) % 4, rest // 16
    return a, (3 * a + b) % 4, (a + 2 * b + c) % 4, core


def partner(me, step):
    core, rest = rem(step, 2), div(step, 2)
    a, b, c = rem(rest, 4), rem(div(rest, 4), 4), div(rest, 16)
    x, y = rem(me[1] + 3 * a + b, 4), rem(me[2] + a + 2 * b + c, 4)
    return rem(me[0] + a, 4), x * 8 + y * 2 + rem(me[3] + core, 2)


def near_partner(me, u):
    return rem(me[0] + div(u, 2), 4), me[1] * 8 + me[2] * 2 + rem(me[3] + rem(u, 2), 2)


def far_partner(me, w):
    return me[0], rem(me[1] + div(w, 4), 4) * 8 + rem(me[2] + rem(w, 4), 4) * 2 + me[3]


def permutations():
    first, second, third = [np.zeros((TOTAL, TOTAL), np.float32) for _ in range(3)]
    for step in range(TOTAL):
        dz, dx, dy, dc = offset_of(step)
        u, w = dz * 2 + dc, dx * 4 + dy
        first[u * OTHERS + w, step] = 1
        second[w * GROUPS + u, u * OTHERS + w] = 1
        third[w * GROUPS + u, step] = 1
    return [jnp.asarray(m, BF16) for m in (first, second, third)]


def dot(a, b):
    return jnp.dot(a, b, preferred_element_type=F32)


def iota(shape, dim):
    return lax.broadcasted_iota(jnp.int32, shape, dim)


def loop(first, last, body, unroll=1):
    def step(n, carry):
        body(n)
        return carry

    lax.fori_loop(first, last, step, 0, unroll=unroll)


def row_slots(me, owner, live):
    rows = owner.shape[1]
    dz = ((owner >> 5) - me[0]) & 3
    dx = ((owner >> 3) - me[1]) & 3
    dy = ((owner >> 1) - me[2]) & 3
    dc = (owner - me[3]) & 1
    b = (dx - 3 * dz) & 3
    c = (dy - dz - 2 * b) & 3
    step = ((c * 4 + b) * 4 + dz) * 2 + dc
    step = jnp.where(iota((1, rows), 1) < live, step, -1)
    marks = (step == iota((TOTAL, rows), 0)).astype(F32)
    width = 256
    upper = (iota((width, width), 0) <= iota((width, width), 1)).astype(BF16)
    carry = jnp.zeros((TOTAL, 1), F32)
    ranks = []
    for block in range(rows // width):
        part = marks[:, block * width : (block + 1) * width]
        running = dot(part.astype(BF16), upper) + carry
        carry = running[:, width - 1 : width]
        ranks.append(jnp.sum(running * part, axis=0, keepdims=True) - 1.0)
    return step.astype(F32), jnp.concatenate(ranks, axis=1)


def fact_sheet(step, rank, angles, transm, tile):
    rows = step.shape[1]
    sines, cosines = jnp.sin(angles), jnp.cos(angles)
    polar_sin = sines[0:1]
    normal_x = polar_sin * cosines[1:2]
    normal_y = polar_sin * sines[1:2]
    normal_z = cosines[0:1]
    facts = [
        transm * (1.0 - normal_x * normal_x),
        transm * (1.0 - normal_y * normal_y),
        transm * (1.0 - normal_z * normal_z),
        -transm * normal_x * normal_y,
        -transm * normal_x * normal_z,
        -transm * normal_y * normal_z,
        (tile >> 8).astype(F32),
        (tile & 255).astype(F32),
    ]
    marks = (step == iota((TOTAL, rows), 0).astype(F32)).astype(F32).astype(BF16)
    chosen = (rank == iota((32, rows), 0).astype(F32)).astype(F32)
    spread = jnp.concatenate([chosen * fact for fact in facts], axis=0).astype(BF16)
    return lax.dot_general(marks, spread, (((1,), (1,)), ((), ())), preferred_element_type=F32)


def swap_groups(values):
    lane = iota(values[0].shape, 1)
    for size in (4, 2, 1):
        high = (lane // (16 * size)) % 2 == 1
        other = jnp.where(high, lane - 16 * size, lane + 16 * size)
        result = list(values)
        for i in range(8):
            if i & size == 0:
                low, up = values[i], values[i + size]
                crossed = jnp.take_along_axis(jnp.where(high, low, up), other, axis=1)
                result[i] = jnp.where(high, crossed, low)
                result[i + size] = jnp.where(high, up, crossed)
        values = result
    return values


def split_lanes(values):
    lane = iota(values[0].shape, 1)
    index = (lane % 16) * 8 + lane // 16
    return swap_groups([jnp.take_along_axis(value, index, axis=1) for value in values])


def join_lanes(values):
    lane = iota(values[0].shape, 1)
    index = (lane % 8) * 16 + lane // 8
    return [jnp.take_along_axis(value, index, axis=1) for value in swap_groups(values)]


def lanes_of(half, m):
    return slice((half * 8 + m) * LANES, (half * 8 + m + 1) * LANES)


def along_x(rows, first, last):
    shape = rows.shape
    rows = rows.reshape(shape[0], 8, 8, LANES)
    lane, l = iota(first.shape, 2), iota(rows.shape, 2)
    edge = jnp.zeros((1,) + first.shape[1:], F32)
    over = pltpu.roll(first, LANES - 1, 2)
    over = jnp.where(lane == LANES - 1, jnp.concatenate([over[1:], edge], axis=0), over)
    under = pltpu.roll(last, 1, 2)
    under = jnp.where(lane == 0, jnp.concatenate([edge, under[:-1]], axis=0), under)
    over = jnp.stack([pltpu.roll(over, 7 - k, 1) if k < 7 else over for k in range(8)], axis=1)
    under = jnp.stack([pltpu.roll(under, 8 - k, 1) if k else under for k in range(8)], axis=1)
    more = jnp.where(l == 7, over, pltpu.roll(rows, 7, 2))
    less = jnp.where(l == 0, under, pltpu.roll(rows, 1, 2))
    return more.reshape(shape), less.reshape(shape)


def along_x_faces(rows):
    lane, l = iota(rows.shape, 3), iota(rows.shape, 2)
    edge = jnp.zeros((rows.shape[0], 1) + rows.shape[2:], F32)
    up, down = pltpu.roll(rows, 7, 2), pltpu.roll(rows, 1, 2)
    over = pltpu.roll(up, LANES - 1, 3)
    over = jnp.where(lane == LANES - 1, jnp.concatenate([over[:, 1:], edge], axis=1), over)
    under = pltpu.roll(down, 1, 3)
    under = jnp.where(lane == 0, jnp.concatenate([edge, under[:, :-1]], axis=1), under)
    return jnp.where(l == 7, over, up), jnp.where(l == 0, under, down)


def at8(start, size):
    return pl.ds(start if isinstance(start, int) else pl.multiple_of(start, 8), size)


def kernel(
    angles_ref,
    transm_ref,
    owner_ref,
    tile_ref,
    live_ref,
    first_ref,
    second_ref,
    third_ref,
    areas_hbm,
    rock_hbm,
    source_hbm,
    start_hbm,
    perm_ref,
    pressure_ref,
    slot_ref,
    send_ref,
    recv_ref,
    near_out,
    near_in,
    far_out,
    far_in,
    turned_ref,
    acc_ref,
    rock_ref,
    source_ref,
    p_ref,
    yy_ref,
    zz_ref,
    load_sem,
    send_sem,
    recv_sem,
    near_send,
    near_recv,
    far_send,
    far_recv,
    halo_send,
    halo_recv,
    coef_send,
    coef_recv,
    ready_sem,
):
    me = place()
    z, h = lax.axis_index("gz"), lax.axis_index("xy")
    gz_count, xy_count = 4, 32
    nz, ny = rock_ref.shape[0], rock_ref.shape[2] // 8

    def beside(dz, dh):
        return (z + dz + gz_count) % gz_count, (h + dh + xy_count) % xy_count

    sides = [(dz, dh) for dz in (-1, 0, 1) for dh in (-1, 0, 1) if dz or dh]

    def planes(d, halo):
        if d == 0:
            return pl.ds(1, nz)
        if halo:
            return pl.ds(0, 1) if d > 0 else pl.ds(nz + 1, 1)
        return pl.ds(nz, 1) if d > 0 else pl.ds(1, 1)

    def lines(d, halo):
        if d == 0:
            return pl.ds(8, ny * 8)
        if halo:
            return pl.ds(0, 8) if d > 0 else pl.ds(ny * 8 + 8, 8)
        return pl.ds(ny * 8, 8) if d > 0 else pl.ds(8, 8)

    def halo_copy(t, n):
        dz, dh = sides[n]
        return pltpu.make_async_remote_copy(
            p_ref.at[t, planes(dz, False), :, lines(dh, False)],
            p_ref.at[t, planes(dz, True), :, lines(dh, True)],
            halo_send.at[t, n],
            halo_recv.at[t, n],
            device_id=beside(dz, dh),
            device_id_type=MESH,
        )

    def drain(ref, first, count, sem):
        part = ref.at[pl.ds(first, count)]
        pltpu.make_async_copy(part, part, sem).wait()

    def collect(areas_ref, plain_ref, picked_ref, column_ref, cell_ref, flip_ref):
        loads = [
            pltpu.make_async_copy(source, target, load_sem.at[n])
            for n, (source, target) in enumerate((
                (areas_hbm, areas_ref),
                (rock_hbm, plain_ref.at[0]),
                (source_hbm, plain_ref.at[1]),
                (start_hbm, plain_ref.at[2]),
            ))
        ]
        for load in loads:
            load.start()

        barrier = pltpu.get_barrier_semaphore()

        def greet(sem, to):
            pl.semaphore_signal(sem, inc=1, device_id=to, device_id_type=MESH)

        loop(1, GROUPS, lambda u: greet(barrier, near_partner(me, u)))
        loop(1, OTHERS, lambda w: greet(barrier, far_partner(me, w)))
        step, rank = row_slots(me, owner_ref[...], live_ref[...])
        slot_ref[0:1] = jnp.where(step >= 0, step * CAP + rank, -1.0)
        slot_ref[1:2] = step
        slot_ref[2:3] = rank
        rows = areas_ref.shape[0]

        def pick(chunk):
            base = chunk * SEND_STEPS
            wanted = (iota((SEND_STEPS * CAP, rows), 0) + base * CAP).astype(F32)
            chosen = (slot_ref[0:1] == wanted).astype(F32).astype(BF16)
            picked_ref[...] = dot(chosen, areas_ref[...])

            def pack(index):
                block = picked_ref[at8(index * CAP, CAP), :]
                parts = [block[:, c * LANES : (c + 1) * LANES] for c in range(CUTS)]
                send_ref[base + index] = jnp.concatenate(parts, axis=0).astype(BF16)

            loop(0, SEND_STEPS, pack, unroll=4)

        def send(step, part):
            pltpu.make_async_remote_copy(
                send_ref.at[step],
                recv_ref.at[step],
                send_sem,
                recv_sem.at[part],
                device_id=partner(me, step),
                device_id_type=MESH,
            ).start()

        def near_copy(u):
            pltpu.make_async_remote_copy(
                near_out.at[u],
                near_in.at[u],
                near_send,
                near_recv,
                device_id=near_partner(me, u),
                device_id_type=MESH,
            ).start()

        def far_copy(w):
            pltpu.make_async_remote_copy(
                far_out.at[w],
                far_in.at[w],
                far_send,
                far_recv,
                device_id=far_partner(me, w),
                device_id_type=MESH,
            ).start()

        pl.semaphore_wait(barrier, GROUPS + OTHERS - 2)
        loop(1, OTHERS, lambda w: greet(ready_sem, far_partner(me, w)))
        loads[0].wait()
        pick(0)
        sheet = fact_sheet(
            slot_ref[1:2], slot_ref[2:3], angles_ref[...], transm_ref[...], tile_ref[...]
        )
        near_out[...] = dot(first_ref[...], sheet.astype(BF16)).reshape(near_out.shape)
        pl.semaphore_wait(ready_sem, OTHERS - 1)
        loop(1, GROUPS, near_copy)
        near_in[0] = near_out[0]
        loop(1, SEND_STEPS, lambda step: send(step, 0))
        recv_ref[0] = send_ref[0]
        def pick_and_send(chunk, part):
            pick(chunk)
            loop(0, SEND_STEPS, lambda index: send(chunk * SEND_STEPS + index, part))

        pick_and_send(1, 0)
        drain(near_in, 1, GROUPS - 1, near_recv)
        swapped = dot(second_ref[...], near_in[...].reshape(TOTAL, 256).astype(BF16))
        far_out[...] = swapped.reshape(far_out.shape)
        loop(1, OTHERS, far_copy)
        far_in[0] = far_out[0]
        loop(2, 6, lambda chunk: pick_and_send(chunk, div(chunk, 2)))
        loop(6, 8, lambda chunk: pick_and_send(chunk, chunk - 3))

        for load in loads[1:]:
            load.wait()

        def split(i):
            for n in range(3):
                spots = [(b, half) for b in range(BANDS) for half in range(HALVES)]
                pieces = []
                for m in range(8):
                    parts = [plain_ref[n, i, b * 8 : (b + 1) * 8, lanes_of(half, m)] for b, half in spots]
                    pieces.append(jnp.concatenate(parts, axis=0))
                for l, value in enumerate(split_lanes(pieces)):
                    for k, (b, half) in enumerate(spots):
                        here = value[k * 8 : (k + 1) * 8]
                        if n == 2:
                            p_ref[0, 1 + i, half, pl.ds(8 + b * 64 + l, 8, stride=8), :] = here
                        else:
                            target = (rock_ref, source_ref)[n]
                            target[i, half, pl.ds(b * 64 + l, 8, stride=8), :] = here

        loop(0, nz, split)

        for n in range(len(sides)):
            halo_copy(0, n).start()

        drain(far_in, 1, OTHERS - 1, far_recv)
        turned_ref[...] = dot(
            jnp.transpose(far_in[...].reshape(TOTAL, 256)).astype(BF16), third_ref[...]
        )
        acc_ref[...] = jnp.zeros_like(acc_ref)
        pieces = acc_ref.shape[0] // 6

        def list_columns(base, count):
            lined = pltpu.roll(turned_ref[...], (TOTAL - base) % TOTAL, 1)
            for index in range(count):
                part = lined[:, index : index + 1]
                where = slice(index * CAP, (index + 1) * CAP)
                for v in range(6):
                    column_ref[v, where, :] = jnp.broadcast_to(part[32 * v : 32 * v + CAP], (CAP, LANES))
                number = part[192 : 192 + CAP] * 256.0 + part[224 : 224 + CAP]
                column_ref[6, where, :] = jnp.broadcast_to(number, (CAP, LANES))

        def add_rows(base, count):
            depth = count * CAP

            def unpack(index):
                block = recv_ref[base + index].astype(F32)
                for c in range(CUTS):
                    cell_ref[c, at8(index * CAP, CAP), :] = block[c * CAP : (c + 1) * CAP]

            loop(0, count, unpack, unroll=4)
            for c in range(CUTS):
                flip_ref[c * LANES : (c + 1) * LANES, :depth] = jnp.transpose(cell_ref[c, :depth]).astype(BF16)

            def component(q):
                lane = iota((depth, LANES), 1).astype(F32)
                number = column_ref[6, :depth]
                value = column_ref[q, :depth]
                parts = [
                    jnp.where(number == lane + part * LANES, value, 0.0).astype(BF16)
                    for part in range(pieces)
                ]
                product = dot(flip_ref[:, :depth], jnp.concatenate(parts, axis=1))
                for part in range(pieces):
                    acc_ref[q * pieces + part] += product[:, part * LANES : (part + 1) * LANES]

            loop(0, 6, component, unroll=2)

        base = 0
        for part, count in enumerate(RECV_STEPS):
            first = 1 if part == 0 else 0
            list_columns(base, count)
            drain(recv_ref, base + first, count - first, recv_sem.at[part])
            add_rows(base, count)
            base += count

    pl.run_scoped(
        collect,
        pltpu.VMEM(areas_hbm.shape, BF16),
        pltpu.VMEM((3,) + rock_hbm.shape, F32),
        pltpu.VMEM((SEND_STEPS * CAP, CELLS), F32),
        pltpu.VMEM((7, DEPTH, LANES), F32),
        pltpu.VMEM((CUTS, DEPTH, LANES), F32),
        pltpu.VMEM((CELLS, DEPTH), BF16),
    )

    def solve(d_ref, g_ref, coef_ref, field_ref):
        def fill(n):
            i, b = div(n, BANDS), rem(n, BANDS)
            rock = rock_ref[i, :, at8(b * 64, 64), :]
            for q in range(3):
                where = pl.ds((q * BANDS + b) * HALVES, HALVES)
                value = acc_ref[where, at8(i * 64, 64), :] + rock
                acc_ref[where, at8(i * 64, 64), :] = value
                if q == 1:
                    yy_ref[i, :, at8(8 + b * 64, 64), :] = value
                if q == 2:
                    zz_ref[1 + i, :, at8(b * 64, 64), :] = value

        loop(0, nz * BANDS, fill)
        coef_copies = []
        for d in (1, -1):
            ends = [
                (yy_ref.at[:, :, lines(d, False)], yy_ref.at[:, :, lines(d, True)], (0, d)),
                (zz_ref.at[planes(d, False)], zz_ref.at[planes(d, True)], (d, 0)),
            ]
            for source, target, side in ends:
                n = len(coef_copies)
                coef_copies.append(
                    pltpu.make_async_remote_copy(
                        source,
                        target,
                        coef_send.at[n],
                        coef_recv.at[n],
                        device_id=beside(*side),
                        device_id_type=MESH,
                    )
                )
        for copy in coef_copies:
            copy.start()

        def join(i, q):
            per = BANDS * HALVES
            values = join_lanes([
                acc_ref[q * per : (q + 2) * per, pl.ds(i * 64 + l, 8, stride=8), :].reshape(16 * per, LANES)
                for l in range(8)
            ])
            for k in range(2 * per):
                b, half = (k % per) // HALVES, k % HALVES
                for m, value in enumerate(values):
                    perm_ref[q + k // per, i, b * 8 : (b + 1) * 8, lanes_of(half, m)] = value[k * 8 : (k + 1) * 8]

        loop(0, nz, lambda i: join(i, 0))
        loop(0, nz // 2, lambda i: join(i, 2))
        for copy in coef_copies:
            copy.wait()

        def clear(ref, index):
            ref[index] = jnp.zeros_like(ref[index])

        every = slice(None)
        low, high = slice(0, 8), slice(ny * 8 + 8, ny * 8 + 16)
        inside = slice(1, nz + 1)

        @pl.when(z == 0)
        def _():
            clear(zz_ref, 0)

        @pl.when(z == gz_count - 1)
        def _():
            clear(zz_ref, nz + 1)

        @pl.when(h == 0)
        def _():
            clear(yy_ref, (every, every, low))

        @pl.when(h == xy_count - 1)
        def _():
            clear(yy_ref, (every, every, high))

        def prepare(n):
            i, b = div(n, BANDS), rem(n, BANDS)
            here = at8(b * 64, 64)
            where = pl.ds(b * HALVES, HALVES)
            k = acc_ref[where, at8(i * 64, 64), :]
            first = acc_ref[where, pl.ds(i * 64, 8, stride=8), :]
            last = acc_ref[where, pl.ds(i * 64 + 7, 8, stride=8), :]
            more, less = along_x(k, first, last)
            faces = [0.5 * (k + more), 0.5 * (k + less)]
            k = yy_ref[i, :, at8(b * 64 + 8, 64), :]
            faces += [0.5 * (k + yy_ref[i, :, at8(b * 64 + 16, 64), :]), 0.5 * (k + yy_ref[i, :, here, :])]
            k = zz_ref[1 + i, :, here, :]
            faces += [0.5 * (k + zz_ref[2 + i, :, here, :]), 0.5 * (k + zz_ref[i, :, here, :])]
            inverse = 1.0 / functools.reduce(lambda left, right: left + right, faces)
            for m, face in enumerate(faces):
                coef_ref[m, i, :, here, :] = face * inverse
            for m in range(3):
                cross = acc_ref[pl.ds(((3 + m) * BANDS + b) * HALVES, HALVES), at8(i * 64, 64), :]
                coef_ref[6 + m, i, :, here, :] = cross * (0.25 * inverse)
            coef_ref[9, i, :, here, :] = source_ref[i, :, here, :] * inverse

        loop(0, nz * BANDS, prepare)

        for t, weight in enumerate(STEP_WEIGHTS * SWEEPS):

            def rows_along_x(i, b, t=t):
                start = 8 + b * 64
                rows = p_ref[t, i, :, at8(start, 64), :]
                first = p_ref[t, i, :, pl.ds(start, 8, stride=8), :]
                last = p_ref[t, i, :, pl.ds(start + 7, 8, stride=8), :]
                return along_x(rows, first, last)

            def inner(i):
                for b in range(BANDS):
                    here = slice(b * 64, b * 64 + 64)
                    more, less = rows_along_x(1 + i, b)
                    d_ref[1 + i, :, 8 + b * 64 : 72 + b * 64, :] = more - less
                    g_ref[i, :, here, :] = (
                        coef_ref[9, i, :, here, :]
                        + coef_ref[0, i, :, here, :] * more
                        + coef_ref[1, i, :, here, :] * less
                    )

            def advance(n, t=t, weight=weight):
                i, y = div(n, ny // SOME), rem(n, ny // SOME) * SOME
                here = at8(y * 8, SOME * 8)
                p = lambda dz, dy: p_ref[t, i + 1 + dz, :, at8((y + 1 + dy) * 8, SOME * 8), :]
                d = lambda dz, dy: d_ref[i + 1 + dz, :, at8((y + 1 + dy) * 8, SOME * 8), :]
                coef = lambda m: coef_ref[m, i, :, here, :]
                total = g_ref[i, :, here, :]
                total = total + coef(2) * p(0, 1) + coef(3) * p(0, -1)
                total = total + coef(4) * p(1, 0) + coef(5) * p(-1, 0)
                total = total + coef(6) * (d(0, 1) - d(0, -1)) + coef(7) * (d(1, 0) - d(-1, 0))
                total = total + coef(8) * ((p(1, 1) - p(-1, 1)) - (p(1, -1) - p(-1, -1)))
                value = (1.0 - weight) * p(0, 0) + weight * total
                if t + 1 < STEPS:
                    p_ref[t + 1, i + 1, :, at8(y * 8 + 8, SOME * 8), :] = value
                else:
                    field_ref[i, :, here, :] = value

            per = ny // SOME
            loop(0, nz, inner)
            if t:
                loop(t * 2 - 2, t * 2, lambda i: join(i, 4))
            for n, side in enumerate(sides):
                if side[0] == 0:
                    halo_copy(t, n).wait()

            @pl.when(h == 0)
            def _():
                clear(p_ref, (t, inside, every, low))

            @pl.when(h == xy_count - 1)
            def _():
                clear(p_ref, (t, inside, every, high))

            for line in (low, high):
                more, less = along_x_faces(p_ref[t, inside, :, line, :])
                d_ref[inside, :, line, :] = more - less
            loop(per, (nz - 1) * per, advance)
            if t == 1:
                loop(nz // 2, nz, lambda i: join(i, 2))
            if t == 2:
                loop(nz - 2, nz, lambda i: join(i, 4))
            for n, side in enumerate(sides):
                if side[0] != 0:
                    halo_copy(t, n).wait()

            @pl.when(h == 0)
            def _():
                clear(p_ref, (t, 0, every, low))
                clear(p_ref, (t, nz + 1, every, low))

            @pl.when(h == xy_count - 1)
            def _():
                clear(p_ref, (t, 0, every, high))
                clear(p_ref, (t, nz + 1, every, high))

            @pl.when(z == 0)
            def _():
                clear(p_ref, (t, 0))

            @pl.when(z == gz_count - 1)
            def _():
                clear(p_ref, (t, nz + 1))

            for i in (0, nz + 1):
                for b in range(BANDS):
                    more, less = rows_along_x(i, b)
                    d_ref[i, :, 8 + b * 64 : 72 + b * 64, :] = more - less
            loop(0, per, advance)
            loop((nz - 1) * per, nz * per, advance)
            if t + 1 < STEPS:
                for n in range(len(sides)):
                    halo_copy(t + 1, n).start()

        def finish(i):
            spots = [(b, half) for b in range(BANDS) for half in range(HALVES)]
            values = join_lanes([
                jnp.concatenate([field_ref[i, half, pl.ds(b * 64 + l, 8, stride=8), :] for b, half in spots], axis=0)
                for l in range(8)
            ])
            for k, (b, half) in enumerate(spots):
                for m, value in enumerate(values):
                    pressure_ref[i, b * 8 : (b + 1) * 8, lanes_of(half, m)] = value[k * 8 : (k + 1) * 8]

        loop(0, nz, finish)
        drain(send_ref, 1, TOTAL - 1, send_sem)
        drain(near_out, 1, GROUPS - 1, near_send)
        drain(far_out, 1, OTHERS - 1, far_send)

    pl.run_scoped(
        solve,
        pltpu.VMEM(p_ref.shape[1:], F32),
        pltpu.VMEM(rock_ref.shape, F32),
        pltpu.VMEM((10,) + rock_ref.shape, F32),
        pltpu.VMEM(rock_ref.shape, F32),
    )


def export_kernel(perm_ref, pressure_ref, perm_out, pressure_out, sems):
    copies = [
        pltpu.make_async_copy(perm_ref.at[q], perm_out.at[q], sems.at[q]) for q in range(6)
    ] + [pltpu.make_async_copy(pressure_ref, pressure_out, sems.at[6])]
    for copy in copies:
        copy.start()
    for copy in copies:
        copy.wait()


def body(areas, angles, transm, owner, tile, live_count, rock, source, start):
    rows = areas.shape[0]
    nz, ny, nx = rock.shape
    lines = ny * 8
    vmem = pl.BlockSpec(memory_space=pltpu.VMEM)
    anywhere = pl.BlockSpec(memory_space=pl.ANY)
    block = (TOTAL, CAP * CUTS, LANES)
    brick = (nz, HALVES, lines, LANES)
    dma = pltpu.SemaphoreType.DMA
    perm, pressure = pl.pallas_call(
        kernel,
        out_shape=[
            pltpu.VMEM((6, nz, ny, nx), F32),
            pltpu.VMEM((nz, ny, nx), F32),
        ],
        in_specs=[vmem] * 8 + [pl.BlockSpec(memory_space=pltpu.HBM)] * 4,
        out_specs=[vmem, vmem],
        scratch_shapes=[
            pltpu.VMEM((8, rows), F32),
            pltpu.VMEM(block, BF16),
            pltpu.VMEM(block, BF16),
            pltpu.VMEM((GROUPS, OTHERS, 256), F32),
            pltpu.VMEM((GROUPS, OTHERS, 256), F32),
            pltpu.VMEM((OTHERS, GROUPS, 256), F32),
            pltpu.VMEM((OTHERS, GROUPS, 256), F32),
            pltpu.VMEM((256, TOTAL), F32),
            pltpu.VMEM((6 * BANDS * HALVES, CELLS, LANES), F32),
            pltpu.VMEM(brick, F32),
            pltpu.VMEM(brick, F32),
            pltpu.VMEM((STEPS, nz + 2, HALVES, lines + 16, LANES), F32),
            pltpu.VMEM((nz, HALVES, lines + 16, LANES), F32),
            pltpu.VMEM((nz + 2, HALVES, lines, LANES), F32),
            dma((4,)),
            dma,
            dma((len(RECV_STEPS),)),
            dma,
            dma,
            dma,
            dma,
            dma((STEPS, 8)),
            dma((STEPS, 8)),
            dma((4,)),
            dma((4,)),
            pltpu.SemaphoreType.REGULAR,
        ],
        compiler_params=pltpu.CompilerParams(
            collective_id=0, has_side_effects=True, vmem_limit_bytes=LIMIT << 20
        ),
    )(
        angles,
        transm.reshape(1, rows),
        owner.reshape(1, rows),
        tile.reshape(1, rows),
        live_count.reshape(1, 1),
        *permutations(),
        areas,
        rock,
        source,
        start,
    )
    return tuple(
        pl.pallas_call(
            export_kernel,
            out_shape=[jax.ShapeDtypeStruct(value.shape, F32) for value in (perm, pressure)],
            in_specs=[vmem, vmem],
            out_specs=[anywhere, anywhere],
            scratch_shapes=[dma((7,))],
            compiler_params=pltpu.CompilerParams(vmem_limit_bytes=8 << 20),
        )(perm, pressure)
    )


def solution(mesh):
    return jax.shard_map(
        body,
        mesh=mesh,
        in_specs=(
            P(("gz", "xy"), None),
            P(None, ("gz", "xy")),
            P(("gz", "xy")),
            P(("gz", "xy"), None),
            P(("gz", "xy")),
            P(("gz", "xy")),
            P("gz", "xy", None),
            P("gz", "xy", None),
            P("gz", "xy", None),
        ),
        out_specs=(P(None, "gz", "xy", None), P("gz", "xy", None)),
        check_vma=False,
    )
```

time: 322 us -> 101 us (0.31)
  Pallas kernels: 320 us -> 99.2 us
    pallas_call x1, Pallas kernels: 224 us -> 3.05 us  [body(): pl.pallas_call(export_kernel, out_shape=[jax.ShapeDtypeStruct(value.shape...]
where the time goes in v2:
time: 101 us
  Pallas kernels  99.2 us (98%)
  between operations  1.45 us (1%)
    pallas_call x1, Pallas kernels, body(): pl.pallas_call(kernel, out_shape=[pltpu.VMEM((6, nz, ny, nx), F32), pltpu...  96.2 us
    pallas_call x1, Pallas kernels, body(): pl.pallas_call(export_kernel, out_shape=[jax.ShapeDtypeStruct(value.shape...  3.05 us

profile of v2, /device:TPU:1, one launch (start us, length us, event | category | flops | bytes accessed | tf_op | source)
XLA Modules:
  0.0 100.7 jit_solution(621690566634872366)
XLA Ops:
  1.3 96.2 %shard_map.131 = (f32[6,8,16,2048]{3,2,1,0:T(8,128)S(1)}, f32[8,16,2048]{2,1,0:T(8,128)S(1)}) custom-call(f32[2,2048]{1,0:T(2,128)} %angles_ref.1, f32[1,2048]{1,0:T(1,128)} %bitcast.5, s32[1,2048]{1,0:T(1,128)} %bitcast.6, s32[1,2048]{1,0:T(1,128)} %bitcast.7, s32[1,1]{1,0:T(1,128)} %bitcast.4.live_ref, bf16[128,128]{1,0:T(8,128)(2,1)} %constant.6.clone.first_ref, ...), custom_call_target="tpu_custom_call" | custom-call | tf_op jit(solution)/shard_map/pallas_call | solution.py:705
  97.5 3.0 %shard_map.132 = (f32[6,8,16,2048]{3,2,1,0:T(8,128)}, f32[8,16,2048]{2,1,0:T(8,128)}) custom-call(f32[6,8,16,2048]{3,2,1,0:T(8,128)S(1)} %get-tuple-element.4.perm_ref, f32[8,16,2048]{2,1,0:T(8,128)S(1)} %get-tuple-element.5.pressure_ref), custom_call_target="tpu_custom_call" | custom-call | tf_op jit(solution)/shard_map/pallas_call | solution.py:757

commit v3 on v2

--- a/solution.py
+++ b/solution.py
@@ -358,29 +358,30 @@
                 device_id_type=MESH,
             ).start()
 
-        pl.semaphore_wait(barrier, GROUPS + OTHERS - 2)
-        loop(1, OTHERS, lambda w: greet(ready_sem, far_partner(me, w)))
-        loads[0].wait()
-        pick(0)
         sheet = fact_sheet(
             slot_ref[1:2], slot_ref[2:3], angles_ref[...], transm_ref[...], tile_ref[...]
         )
         near_out[...] = dot(first_ref[...], sheet.astype(BF16)).reshape(near_out.shape)
-        pl.semaphore_wait(ready_sem, OTHERS - 1)
+        pl.semaphore_wait(barrier, GROUPS + OTHERS - 2)
+        loop(1, OTHERS, lambda w: greet(ready_sem, far_partner(me, w)))
         loop(1, GROUPS, near_copy)
         near_in[0] = near_out[0]
+        loads[0].wait()
+        pick(0)
+        drain(near_in, 1, GROUPS - 1, near_recv)
+        swapped = dot(second_ref[...], near_in[...].reshape(TOTAL, 256).astype(BF16))
+        far_out[...] = swapped.reshape(far_out.shape)
+        far_in[0] = far_out[0]
+        pl.semaphore_wait(ready_sem, OTHERS - 1)
         loop(1, SEND_STEPS, lambda step: send(step, 0))
         recv_ref[0] = send_ref[0]
+
         def pick_and_send(chunk, part):
             pick(chunk)
             loop(0, SEND_STEPS, lambda index: send(chunk * SEND_STEPS + index, part))
 
         pick_and_send(1, 0)
-        drain(near_in, 1, GROUPS - 1, near_recv)
-        swapped = dot(second_ref[...], near_in[...].reshape(TOTAL, 256).astype(BF16))
-        far_out[...] = swapped.reshape(far_out.shape)
         loop(1, OTHERS, far_copy)
-        far_in[0] = far_out[0]
         loop(2, 6, lambda chunk: pick_and_send(chunk, div(chunk, 2)))
         loop(6, 8, lambda chunk: pick_and_send(chunk, chunk - 3))
 

time: 101 us -> 95 us (0.941)
  Pallas kernels: 99.2 us -> 93.1 us
    pallas_call x1, Pallas kernels: 96.2 us -> 90.1 us  [body(): pl.pallas_call(kernel, out_shape=[pltpu.VMEM((6, nz, ny, nx), F32), pltpu...]
where the time goes in v3:
time: 95 us; the launch traced here: 94.6 us
  Pallas kernels  93.1 us (98%)
  between operations  1.45 us (2%)
    pallas_call x1, Pallas kernels, body(): pl.pallas_call(kernel, out_shape=[pltpu.VMEM((6, nz, ny, nx), F32), pltpu...  90.1 us
    pallas_call x1, Pallas kernels, body(): pl.pallas_call(export_kernel, out_shape=[jax.ShapeDtypeStruct(value.shape...  3.05 us

profile of v3, /device:TPU:1, one launch (start us, length us, event | category | flops | bytes accessed | tf_op | source)
XLA Modules:
  0.0 94.6 jit_solution(7036016643238546045)
XLA Ops:
  1.3 90.1 %shard_map.131 = (f32[6,8,16,2048]{3,2,1,0:T(8,128)S(1)}, f32[8,16,2048]{2,1,0:T(8,128)S(1)}) custom-call(f32[2,2048]{1,0:T(2,128)} %angles_ref.1, f32[1,2048]{1,0:T(1,128)} %bitcast.5, s32[1,2048]{1,0:T(1,128)} %bitcast.6, s32[1,2048]{1,0:T(1,128)} %bitcast.7, s32[1,1]{1,0:T(1,128)} %bitcast.4.live_ref, bf16[128,128]{1,0:T(8,128)(2,1)} %constant.6.clone.first_ref, ...), custom_call_target="tpu_custom_call" | custom-call | tf_op jit(solution)/shard_map/pallas_call | solution.py:706
  91.4 3.0 %shard_map.132 = (f32[6,8,16,2048]{3,2,1,0:T(8,128)}, f32[8,16,2048]{2,1,0:T(8,128)}) custom-call(f32[6,8,16,2048]{3,2,1,0:T(8,128)S(1)} %get-tuple-element.4.perm_ref, f32[8,16,2048]{2,1,0:T(8,128)S(1)} %get-tuple-element.5.pressure_ref), custom_call_target="tpu_custom_call" | custom-call | tf_op jit(solution)/shard_map/pallas_call | solution.py:758

commit v4 on v3

--- a/solution.py
+++ b/solution.py
@@ -33,7 +33,7 @@
 CUTS = CELLS // LANES
 HALVES = 2
 BANDS = 2
-SOME = 4
+SOME = 8
 LIMIT = 56
 STEPS = len(STEP_WEIGHTS) * SWEEPS
 
@@ -258,7 +258,7 @@
     def beside(dz, dh):
         return (z + dz + gz_count) % gz_count, (h + dh + xy_count) % xy_count
 
-    sides = [(dz, dh) for dz in (-1, 0, 1) for dh in (-1, 0, 1) if dz or dh]
+    sides = [(-1, 0), (1, 0), (0, -1), (0, 1), (-1, -1), (-1, 1), (1, -1), (1, 1)]
 
     def planes(d, halo):
         if d == 0:

time: 95 us -> 94.2 us (level)
  no operation moved by 1% of the time
where the time goes in v4:
time: 94.2 us; the launch traced here: 93.8 us
  Pallas kernels  92.4 us (98%)
  between operations  1.45 us (2%)
    pallas_call x1, Pallas kernels, body(): pl.pallas_call(kernel, out_shape=[pltpu.VMEM((6, nz, ny, nx), F32), pltpu...  89.4 us
    pallas_call x1, Pallas kernels, body(): pl.pallas_call(export_kernel, out_shape=[jax.ShapeDtypeStruct(value.shape...  3.05 us

profile of v4, /device:TPU:1, one launch (start us, length us, event | category | flops | bytes accessed | tf_op | source)
XLA Modules:
  0.0 93.8 jit_solution(10836638011216515450)
XLA Ops:
  1.3 89.4 %shard_map.131 = (f32[6,8,16,2048]{3,2,1,0:T(8,128)S(1)}, f32[8,16,2048]{2,1,0:T(8,128)S(1)}) custom-call(f32[2,2048]{1,0:T(2,128)} %angles_ref.1, f32[1,2048]{1,0:T(1,128)} %bitcast.5, s32[1,2048]{1,0:T(1,128)} %bitcast.6, s32[1,2048]{1,0:T(1,128)} %bitcast.7, s32[1,1]{1,0:T(1,128)} %bitcast.4.live_ref, bf16[128,128]{1,0:T(8,128)(2,1)} %constant.6.clone.first_ref, ...), custom_call_target="tpu_custom_call" | custom-call | tf_op jit(solution)/shard_map/pallas_call | solution.py:706
  90.6 3.0 %shard_map.132 = (f32[6,8,16,2048]{3,2,1,0:T(8,128)}, f32[8,16,2048]{2,1,0:T(8,128)}) custom-call(f32[6,8,16,2048]{3,2,1,0:T(8,128)S(1)} %get-tuple-element.4.perm_ref, f32[8,16,2048]{2,1,0:T(8,128)S(1)} %get-tuple-element.5.pressure_ref), custom_call_target="tpu_custom_call" | custom-call | tf_op jit(solution)/shard_map/pallas_call | solution.py:758
